TPU v7x, 32 devices: a whole 2x2x4 slice. The times are simulated.
32 devices in a mesh: groups: 2 (over y), leaf: 4 (over z), sub: 2 (over x), col: 2 (over core).
Axes of the slice: x: 2, y: 2, z: 4, core: 2. Of those that a mesh axis runs over, the one named last changes fastest.
Arguments:
- incident: bfloat16 [2, 4096, 2048], P(None, ('leaf', 'sub'), ('groups', 'col')), parts along dimension 2, may hold values from -6 to 6
- self_weight: bfloat16 [10, 2, 32, 128, 128], P('groups', None, ('leaf', 'sub')), parts along dimension 0, may hold values from -0.3125 to 0.3125
- cross_weight: bfloat16 [10, 2, 32, 64, 128], P('groups', None, ('leaf', 'sub')), parts along dimension 0, may hold values from -0.4375 to 0.4375
- coupling: int32 [10, 32], P('groups', ('leaf', 'sub')), parts along dimension 0, may hold values 0 or 1
- block_ranks: int32 [10, 32], P('groups', ('leaf', 'sub')), parts along dimension 0, may hold values from 16 to 64
- leaf_order: int32 [64, 128], P(('groups', 'leaf', 'sub')), parts along dimension 0, may hold values from 0 to 127, each once within a row
Outputs:
- scattered: bfloat16 [2, 4096, 2048], P(None, ('leaf', 'sub'), ('groups', 'col')), parts along dimension 2
There are 2 independent parts, one for each index of `groups`. A program takes and returns all parts, laid end to end along the dimension named above; each array names one. Nothing has to cross between parts.
All inputs are finite; a program needn't handle non-finite values. No bound on the sum of `coupling` on one device may be relied on, other than what follows from the above.
Results may differ from a plain program's by a relative error of at most 0.007.
Values may be sent and summed in bfloat16 or wider, within the bound.
A program may use at most 64 MiB of HBM per device.

v0:
```python
import jax
import jax.numpy as jnp
from jax import lax
from jax.sharding import PartitionSpec as P


def from_partner(x, axis, stride):
    return lax.ppermute(x, axis, [(i, i ^ 1 << stride) for i in range(lax.axis_size(axis))])


def level_matrix(self_weight, cross_weight, coupling, block_ranks, level_index):
    lead_rows = cross_weight.shape[3]
    rank_index = jnp.arange(lead_rows, dtype=jnp.int32)
    coupled = (rank_index[None, :] < block_ranks[level_index][:, None]) & (
        coupling[level_index][:, None] == 1
    )
    masked = cross_weight[level_index] * coupled[None, :, :, None].astype(jnp.bfloat16)
    cross_t = jnp.swapaxes(masked, 2, 3)
    own = self_weight[level_index]
    upper = jnp.concatenate([own[0], -own[1], cross_t[0], -cross_t[1]], axis=2)
    lower = jnp.concatenate([own[1], own[0], cross_t[1], cross_t[0]], axis=2)
    return jnp.concatenate([upper, lower], axis=1)


def apply_level(field, sibling, self_weight, cross_weight, coupling, block_ranks, level_index):
    blocks = field.shape[0]
    block_rows = field.shape[2]
    columns = field.shape[3]
    lead_rows = sibling.shape[2]
    matrix = level_matrix(self_weight, cross_weight, coupling, block_ranks, level_index)
    stacked = jnp.concatenate(
        [
            field.reshape(blocks, 2 * block_rows, columns),
            sibling.reshape(blocks, 2 * lead_rows, columns),
        ],
        axis=1,
    )
    result = jnp.einsum("bij,bjn->bin", matrix, stacked, preferred_element_type=jnp.float32)
    return result.astype(jnp.bfloat16).reshape(blocks, 2, block_rows, columns)


def shards(incident, self_weight, cross_weight, coupling, block_ranks, leaf_order):
    blocks = leaf_order.shape[0]
    block_rows = leaf_order.shape[1]
    columns = incident.shape[2]
    lead_rows = cross_weight.shape[3]
    row_index = jnp.arange(block_rows, dtype=jnp.int32)
    selector = (leaf_order[:, :, None] == row_index[None, None, :]).astype(jnp.bfloat16)
    field = incident.reshape(2, blocks, block_rows, columns)
    field = jnp.einsum(
        "irk,cikn->icrn", selector, field, preferred_element_type=jnp.float32
    ).astype(jnp.bfloat16)
    local_bits = blocks.bit_length() - 1
    sub_bits = lax.axis_size("sub").bit_length() - 1
    leaf_bits = lax.axis_size("leaf").bit_length() - 1
    level_index = 0
    for which_bit in range(local_bits):
        stride = 2**which_bit
        sibling = field.reshape(blocks // (2 * stride), 2, stride, 2, block_rows, columns)[:, ::-1]
        sibling = sibling.reshape(blocks, 2, block_rows, columns)[:, :, :lead_rows]
        field = apply_level(
            field, sibling, self_weight, cross_weight, coupling, block_ranks, level_index
        )
        level_index += 1
    for which_bit in range(sub_bits):
        sibling = from_partner(field, "sub", which_bit)[:, :, :lead_rows]
        field = apply_level(
            field, sibling, self_weight, cross_weight, coupling, block_ranks, level_index
        )
        level_index += 1
    for which_bit in range(leaf_bits):
        sibling = from_partner(field, "leaf", which_bit)[:, :, :lead_rows]
        field = apply_level(
            field, sibling, self_weight, cross_weight, coupling, block_ranks, level_index
        )
        level_index += 1
    field = jnp.transpose(field, (1, 0, 2, 3))
    return field.reshape(2, blocks * block_rows, columns)


def solution(mesh):
    in_specs = (
        P(None, ("leaf", "sub"), ("groups", "col")),
        P("groups", None, ("leaf", "sub"), None, None),
        P("groups", None, ("leaf", "sub"), None, None),
        P("groups", ("leaf", "sub")),
        P("groups", ("leaf", "sub")),
        P(("groups", "leaf", "sub"), None),
    )
    out_specs = P(None, ("leaf", "sub"), ("groups", "col"))
    return jax.shard_map(shards, mesh=mesh, in_specs=in_specs, out_specs=out_specs, check_vma=False)
```

profile of v0, /device:TPU:0, one launch (start us, length us, event | category | flops | bytes accessed | tf_op | source)
XLA Modules:
  0.0 122.0 jit_solution(1719609606258684023)
XLA Ops:
  0.0 1.1 slice_reduce_fusion.4
  1.1 1.6 %fusion.121 = (pred[4]{0:T(512)(128)(4,1)S(1)}, pred[4]{0:T(512)(128)(4,1)S(1)}, pred[4]{0:T(512)(128)(4,1)}, pred[4]{0:T(512)(128)(4,1)S(1)}, pred[4]{0:T(512)(128)(4,1)S(1)}) fusion(s32[5,4]{0,1:T(4,128)} %param.9), kind=kLoop, calls=%fused_computation.152 | loop fusion | flops 20 | bytes 100 | tf_op jit(solution)/shard_map/eq | solution.py:15
  2.7 1.3 %fusion.149 = (bf16[1,2,4,64,128]{4,3,2,1,0:T(8,128)(2,1)S(1)}, bf16[1,2,4,64,128]{4,3,2,1,0:T(8,128)(2,1)S(1)}, bf16[1,2,4,64,128]{4,3,2,1,0:T(8,128)(2,1)S(1)}...) fusion(bf16[5,2,4,64,128]{4,3,2,1,0:T(8,128)(2,1)} %param.8), kind=kLoop, calls=%fused_computation.180 | loop fusion | bytes 1310720 | tf_op jit(solution)/shard_map/slice | solution.py:17
  4.0 0.2 copy.19
  4.2 0.1 fusion.132
  4.3 0.7 slice_bitcast_fusion
  5.0 0.7 fusion.148
  5.7 1.1 slice_bitcast_fusion.18
  6.8 0.9 fusion.139
  7.7 0.2 copy.18
  7.9 0.1 fusion.126
  8.0 0.7 slice_bitcast_fusion.2
  8.7 0.7 fusion.147
  9.4 0.5 convolution_convert_fusion
  9.8 0.1 rev.6
  10.0 2.0 %fusion.32 = bf16[4,256,512]{2,1,0:T(8,128)(2,1)S(1)} fusion(bf16[4,128,512]{2,1,0:T(8,128)(2,1)S(1)} %bitcast.124, bf16[4,256,512]{2,1,0:T(8,128)(2,1)S(1)} %bitcast.118, bf16[4,128,64]{2,1,0:T(8,128)(2,1)} %get-tuple-element.44, bf16[4,128,64]{2,1,0:T(8,128)(2,1)} %get-tuple-element.43, bf16[4,128,128]{2,1,0:T(8,128)(2,1)} %get-tuple-element.29, ...), kind=kOutput, calls=%fused_computation.24 | convolution fusion | flops 412614656 | bytes 3211264 | tf_op jit(solution)/shard_map/bij,bjn->bin/dot_general | solution.py:38
  12.0 0.1 rev.7
  12.1 3.0 %fusion.29 = bf16[4,256,512]{2,1,0:T(8,128)(2,1)} fusion(bf16[4,128,512]{2,1,0:T(8,128)(2,1)S(1)} %bitcast.125, bf16[4,256,512]{2,1,0:T(8,128)(2,1)S(1)} %fusion.32, bf16[4,128,64]{2,1,0:T(8,128)(2,1)} %get-tuple-element.42, bf16[4,128,64]{2,1,0:T(8,128)(2,1)} %get-tuple-element.41, bf16[4,128,128]{2,1,0:T(8,128)(2,1)} %get-tuple-element.22, ...), kind=kOutput, calls=%fused_computation.23 | convolution fusion | flops 412614656 | bytes 3211264 | tf_op jit(solution)/shard_map/bij,bjn->bin/dot_general | solution.py:38
  15.1 2.9 %collective-permute-start = (bf16[4,2,128,512]{3,2,1,0:T(8,128)(2,1)}, bf16[4,2,128,512]{3,2,1,0:T(8,128)(2,1)S(1)}, u32[]{:S(2)}, u32[]{:S(2)}) collective-permute-start(bf16[4,2,128,512]{3,2,1,0:T(8,128)(2,1)} %bitcast.41), channel_id=1, source_target_pairs={{0,2},{2,0},{1,3},{3,1},{4,6},{6,4},{5,7},{7,5},{8,10},{10,8},{9,1... | collective-permute-start | bytes 3145736 | tf_op jit(solution)/shard_map/ppermute | solution.py:8
  18.0 0.2 copy.17
  18.3 23.1 %collective-permute-done = bf16[4,2,128,512]{3,2,1,0:T(8,128)(2,1)S(1)} collective-permute-done((bf16[4,2,128,512]{3,2,1,0:T(8,128)(2,1)}, bf16[4,2,128,512]{3,2,1,0:T(8,128)(2,1)S(1)}, u32[]{:S(2)}, u32[]{:S(2)}) %collective-permute-start) | collective-permute-done | bytes 1048608 | tf_op jit(solution)/shard_map/ppermute | solution.py:8
  41.5 2.9 %fusion.26 = bf16[4,256,512]{2,1,0:T(8,128)(2,1)} fusion(bf16[4,128,512]{2,1,0:T(8,128)(2,1)S(1)} %bitcast.126, bf16[4,256,512]{2,1,0:T(8,128)(2,1)} %fusion.29, bf16[4,128,64]{2,1,0:T(8,128)(2,1)S(1)} %get-tuple-element.40, bf16[4,128,64]{2,1,0:T(8,128)(2,1)S(1)} %get-tuple-element.39, bf16[4,128,128]{2,1,0:T(8,128)(2,1)S(1)} %copy-done.9, ...), kind=kOutput, calls=%fused_computation.22 | convolution fusion | flops 412614656 | bytes 3211264 | tf_op jit(solution)/shard_map/bij,bjn->bin/dot_general | solution.py:38
  44.4 1.8 %collective-permute-start.1 = (bf16[4,2,128,512]{3,2,1,0:T(8,128)(2,1)}, bf16[4,2,128,512]{3,2,1,0:T(8,128)(2,1)S(1)}, u32[]{:S(2)}, u32[]{:S(2)}) collective-permute-start(bf16[4,2,128,512]{3,2,1,0:T(8,128)(2,1)} %bitcast.43), channel_id=1, source_target_pairs={{0,4},{4,0},{8,12},{12,8},{1,5},{5,1},{9,13},{13,9},{2,6},{6,2},{1... | collective-permute-start | bytes 3145736 | tf_op jit(solution)/shard_map/ppermute | solution.py:8
  46.2 0.2 copy.16
  46.4 0.1 fusion.120
  46.6 22.3 %collective-permute-done.1 = bf16[4,2,128,512]{3,2,1,0:T(8,128)(2,1)S(1)} collective-permute-done((bf16[4,2,128,512]{3,2,1,0:T(8,128)(2,1)}, bf16[4,2,128,512]{3,2,1,0:T(8,128)(2,1)S(1)}, u32[]{:S(2)}, u32[]{:S(2)}) %collective-permute-start.1) | collective-permute-done | bytes 1048608 | tf_op jit(solution)/shard_map/ppermute | solution.py:8
  69.0 2.9 %fusion.23 = bf16[4,256,512]{2,1,0:T(8,128)(2,1)} fusion(bf16[4,128,512]{2,1,0:T(8,128)(2,1)S(1)} %bitcast.127, bf16[4,256,512]{2,1,0:T(8,128)(2,1)} %fusion.26, bf16[4,128,64]{2,1,0:T(8,128)(2,1)S(1)} %get-tuple-element.38, bf16[4,128,64]{2,1,0:T(8,128)(2,1)S(1)} %get-tuple-element.37, bf16[4,128,128]{2,1,0:T(8,128)(2,1)S(1)} %copy-done.6, ...), kind=kOutput, calls=%fused_computation.21 | convolution fusion | flops 412614656 | bytes 3211264 | tf_op jit(solution)/shard_map/bij,bjn->bin/dot_general | solution.py:38
  71.9 2.5 %collective-permute-start.2 = (bf16[4,2,128,512]{3,2,1,0:T(8,128)(2,1)}, bf16[4,2,128,512]{3,2,1,0:T(8,128)(2,1)S(1)}, u32[]{:S(2)}, u32[]{:S(2)}) collective-permute-start(bf16[4,2,128,512]{3,2,1,0:T(8,128)(2,1)} %bitcast.45), channel_id=1, source_target_pairs={{0,8},{4,12},{8,0},{12,4},{1,9},{5,13},{9,1},{13,5},{2,10},{6,14},... | collective-permute-start | bytes 3145736 | tf_op jit(solution)/shard_map/ppermute | solution.py:8
  74.5 0.2 copy.15
  74.7 44.2 %collective-permute-done.2 = bf16[4,2,128,512]{3,2,1,0:T(8,128)(2,1)S(1)} collective-permute-done((bf16[4,2,128,512]{3,2,1,0:T(8,128)(2,1)}, bf16[4,2,128,512]{3,2,1,0:T(8,128)(2,1)S(1)}, u32[]{:S(2)}, u32[]{:S(2)}) %collective-permute-start.2) | collective-permute-done | bytes 1048608 | tf_op jit(solution)/shard_map/ppermute | solution.py:8
  119.0 1.9 %fusion.20 = bf16[4,256,512]{2,1,0:T(8,128)(2,1)S(1)} fusion(bf16[4,128,512]{2,1,0:T(8,128)(2,1)S(1)} %bitcast.123, bf16[4,256,512]{2,1,0:T(8,128)(2,1)} %fusion.23, bf16[4,128,64]{2,1,0:T(8,128)(2,1)S(1)} %get-tuple-element.36, bf16[4,128,64]{2,1,0:T(8,128)(2,1)S(1)} %get-tuple-element.35, bf16[4,128,128]{2,1,0:T(8,128)(2,1)S(1)} %copy-done.3, ...), kind=kOutput, calls=%fused_computation.20 | convolution fusion | flops 412614656 | bytes 3211264 | tf_op jit(solution)/shard_map/bij,bjn->bin/dot_general | solution.py:38
  121.0 1.1 copy.13
  (42 shorter events, 0.5 us)
Async XLA Ops:
  0.0 9.4 %copy-start = (bf16[2,512,512]{2,1,0:T(8,128)(2,1)S(1)}, bf16[2,512,512]{2,1,0:T(8,128)(2,1)}, u32[]{:S(2)}) copy-start(bf16[2,512,512]{2,1,0:T(8,128)(2,1)} %param.6) | copy-start | bytes 3145732
  2.7 3.0 %copy-start.1 = (bf16[5,2,4,128,128]{4,3,2,1,0:T(8,128)(2,1)S(1)}, bf16[5,2,4,128,128]{4,3,2,1,0:T(8,128)(2,1)}, u32[]{:S(2)}) copy-start(bf16[5,2,4,128,128]{4,3,2,1,0:T(8,128)(2,1)} %param.7) | copy-start | bytes 3932164
  6.8 2.6 %copy-start.11 = (s32[4,128]{1,0:T(4,128)S(1)}, s32[4,128]{1,0:T(4,128)}, u32[]{:S(2)}) copy-start(s32[4,128]{1,0:T(4,128)} %param.11) | copy-start | bytes 6148
  15.1 26.3 %collective-permute-start = (bf16[4,2,128,512]{3,2,1,0:T(8,128)(2,1)}, bf16[4,2,128,512]{3,2,1,0:T(8,128)(2,1)S(1)}, u32[]{:S(2)}, u32[]{:S(2)}) collective-permute-start(bf16[4,2,128,512]{3,2,1,0:T(8,128)(2,1)} %bitcast.41), channel_id=1, source_target_pairs={{0,2},{2,0},{1,3},{3,1},{4,6},{6,4},{5,7},{7,5},{8,10},{10,8},{9,1... | collective-permute-start | bytes 3145736 | tf_op jit(solution)/shard_map/ppermute | solution.py:8
  18.0 23.4 %copy-start.8 = (bf16[4,128,128]{2,1,0:T(8,128)(2,1)S(1)}, bf16[4,128,128]{2,1,0:T(8,128)(2,1)}, u32[]{:S(2)}) copy-start(bf16[4,128,128]{2,1,0:T(8,128)(2,1)} %get-tuple-element.23) | copy-start | bytes 393220
  18.0 23.4 %copy-start.9 = (bf16[4,128,128]{2,1,0:T(8,128)(2,1)S(1)}, bf16[4,128,128]{2,1,0:T(8,128)(2,1)}, u32[]{:S(2)}) copy-start(bf16[4,128,128]{2,1,0:T(8,128)(2,1)} %get-tuple-element.24) | copy-start | bytes 393220
  18.0 23.4 %copy-start.10 = (bf16[4,128,128]{2,1,0:T(8,128)(2,1)S(1)}, bf16[4,128,128]{2,1,0:T(8,128)(2,1)}, u32[]{:S(2)}) copy-start(bf16[4,128,128]{2,1,0:T(8,128)(2,1)} %get-tuple-element.18) | copy-start | bytes 393220
  41.5 5.0 %copy-start.12 = (pred[4]{0:T(512)(128)(4,1)S(1)}, pred[4]{0:T(512)(128)(4,1)}, u32[]{:S(2)}) copy-start(pred[4]{0:T(512)(128)(4,1)} %get-tuple-element.7) | copy-start | bytes 16
  44.4 24.5 %collective-permute-start.1 = (bf16[4,2,128,512]{3,2,1,0:T(8,128)(2,1)}, bf16[4,2,128,512]{3,2,1,0:T(8,128)(2,1)S(1)}, u32[]{:S(2)}, u32[]{:S(2)}) collective-permute-start(bf16[4,2,128,512]{3,2,1,0:T(8,128)(2,1)} %bitcast.43), channel_id=1, source_target_pairs={{0,4},{4,0},{8,12},{12,8},{1,5},{5,1},{9,13},{13,9},{2,6},{6,2},{1... | collective-permute-start | bytes 3145736 | tf_op jit(solution)/shard_map/ppermute | solution.py:8
  46.2 22.8 %copy-start.5 = (bf16[4,128,128]{2,1,0:T(8,128)(2,1)S(1)}, bf16[4,128,128]{2,1,0:T(8,128)(2,1)}, u32[]{:S(2)}) copy-start(bf16[4,128,128]{2,1,0:T(8,128)(2,1)} %get-tuple-element.25) | copy-start | bytes 393220
  46.2 22.8 %copy-start.6 = (bf16[4,128,128]{2,1,0:T(8,128)(2,1)S(1)}, bf16[4,128,128]{2,1,0:T(8,128)(2,1)}, u32[]{:S(2)}) copy-start(bf16[4,128,128]{2,1,0:T(8,128)(2,1)} %get-tuple-element.26) | copy-start | bytes 393220
  46.2 22.8 %copy-start.7 = (bf16[4,128,128]{2,1,0:T(8,128)(2,1)S(1)}, bf16[4,128,128]{2,1,0:T(8,128)(2,1)}, u32[]{:S(2)}) copy-start(bf16[4,128,128]{2,1,0:T(8,128)(2,1)} %get-tuple-element.19) | copy-start | bytes 393220
  71.9 47.0 %collective-permute-start.2 = (bf16[4,2,128,512]{3,2,1,0:T(8,128)(2,1)}, bf16[4,2,128,512]{3,2,1,0:T(8,128)(2,1)S(1)}, u32[]{:S(2)}, u32[]{:S(2)}) collective-permute-start(bf16[4,2,128,512]{3,2,1,0:T(8,128)(2,1)} %bitcast.45), channel_id=1, source_target_pairs={{0,8},{4,12},{8,0},{12,4},{1,9},{5,13},{9,1},{13,5},{2,10},{6,14},... | collective-permute-start | bytes 3145736 | tf_op jit(solution)/shard_map/ppermute | solution.py:8
  74.5 44.5 %copy-start.2 = (bf16[4,128,128]{2,1,0:T(8,128)(2,1)S(1)}, bf16[4,128,128]{2,1,0:T(8,128)(2,1)}, u32[]{:S(2)}) copy-start(bf16[4,128,128]{2,1,0:T(8,128)(2,1)} %get-tuple-element.20) | copy-start | bytes 393220
  74.5 44.5 %copy-start.3 = (bf16[4,128,128]{2,1,0:T(8,128)(2,1)S(1)}, bf16[4,128,128]{2,1,0:T(8,128)(2,1)}, u32[]{:S(2)}) copy-start(bf16[4,128,128]{2,1,0:T(8,128)(2,1)} %get-tuple-element.27) | copy-start | bytes 393220
  74.5 44.5 %copy-start.4 = (bf16[4,128,128]{2,1,0:T(8,128)(2,1)S(1)}, bf16[4,128,128]{2,1,0:T(8,128)(2,1)}, u32[]{:S(2)}) copy-start(bf16[4,128,128]{2,1,0:T(8,128)(2,1)} %get-tuple-element.15) | copy-start | bytes 393220
where the time goes:
time: 122 us
  waiting for transfers between devices  89.6 us (73%)
  matrix products  13.3 us (11%)
  local copies, waits for them, and re-layouts  7.34 us (6%)
  starting transfers between devices  7.3 us (6%)
  other arithmetic  4.22 us (3%)
    ppermute x3, waiting for transfers between devices, from_partner(): lax.ppermute(x, axis, [(i, i ^ 1 << stride) for i in range(lax.axis_size(...  89.6 us
    dot_general x5, matrix products, apply_level(): jnp.einsum('bij,bjn->bin', matrix, stacked, preferred_element_type=jnp.fl...  12.8 us
    ppermute x3, starting transfers between devices, from_partner(): lax.ppermute(x, axis, [(i, i ^ 1 << stride) for i in range(lax.axis_size(...  7.3 us
    squeeze x6, local copies, waits for them, and re-layouts, level_matrix(): upper = jnp.concatenate([own[0], -own[1], cross_t[0], -cross_t[1]], axis=2)  2.55 us
  transfers between devices with their start and end apart: 3, of which 3 were waited for; matrix products, arithmetic and copies ran while one was open for 1% of the time, Pallas kernels for 0%

commit v1 on v0

--- a/solution.py
+++ b/solution.py
@@ -63,13 +63,13 @@
         )
         level_index += 1
     for which_bit in range(sub_bits):
-        sibling = from_partner(field, "sub", which_bit)[:, :, :lead_rows]
+        sibling = from_partner(field[:, :, :lead_rows], "sub", which_bit)
         field = apply_level(
             field, sibling, self_weight, cross_weight, coupling, block_ranks, level_index
         )
         level_index += 1
     for which_bit in range(leaf_bits):
-        sibling = from_partner(field, "leaf", which_bit)[:, :, :lead_rows]
+        sibling = from_partner(field[:, :, :lead_rows], "leaf", which_bit)
         field = apply_level(
             field, sibling, self_weight, cross_weight, coupling, block_ranks, level_index
         )

time: 122 us -> 73.1 us (0.60)
  waiting for transfers between devices: 89.6 us -> 43.5 us
  matrix products: 13.3 us -> 9.16 us
    ppermute x3, waiting for transfers between devices: 89.6 us -> 43.5 us  [from_partner(): lax.ppermute(x, axis, [(i, i ^ 1 << stride) for i in range(lax.axis_size(...]
    dot_general x5, matrix products: 12.8 us -> 8.68 us  [apply_level(): jnp.einsum('bij,bjn->bin', matrix, stacked, preferred_element_type=jnp.fl...]
  transfers between devices with their start and end apart: 3 -> 3, of which waited for: 3 -> 3; matrix products, arithmetic and copies ran while one was open for 1% -> 2% of each run, Pallas kernels for 0% -> 0%
where the time goes in v1:
time: 73.1 us; the launch traced here: 72.8 us
  waiting for transfers between devices  43.5 us (60%)
  matrix products  9.16 us (13%)
  starting transfers between devices  7.47 us (10%)
  local copies, waits for them, and re-layouts  7.44 us (10%)
  other arithmetic  4.92 us (7%)
    ppermute x3, waiting for transfers between devices, from_partner(): lax.ppermute(x, axis, [(i, i ^ 1 << stride) for i in range(lax.axis_size(...  43.5 us
    dot_general x5, matrix products, apply_level(): jnp.einsum('bij,bjn->bin', matrix, stacked, preferred_element_type=jnp.fl...  8.68 us
    ppermute x3, starting transfers between devices, from_partner(): lax.ppermute(x, axis, [(i, i ^ 1 << stride) for i in range(lax.axis_size(...  7.47 us
    squeeze x6, local copies, waits for them, and re-layouts, level_matrix(): upper = jnp.concatenate([own[0], -own[1], cross_t[0], -cross_t[1]], axis=2)  2.63 us
    neg x6, other arithmetic, level_matrix(): upper = jnp.concatenate([own[0], -own[1], cross_t[0], -cross_t[1]], axis=2)  2.29 us
    eq x1, other arithmetic, level_matrix(): coupling[level_index][:, None] == 1  1.58 us
  transfers between devices with their start and end apart: 3, of which 3 were waited for; matrix products, arithmetic and copies ran while one was open for 2% of the time, Pallas kernels for 0%

profile of v1, /device:TPU:0, one launch (start us, length us, event | category | flops | bytes accessed | tf_op | source)
XLA Modules:
  0.0 72.8 jit_solution(16185727738351417410)
XLA Ops:
  0.0 1.1 %slice_reduce_fusion.4 = (s32[4]{0:T(128)S(1)}, s32[4]{0:T(128)S(1)}, s32[4]{0:T(128)S(1)}, s32[4]{0:T(128)S(1)}, s32[4]{0:T(128)S(1)}) fusion(s32[5,4]{0,1:T(4,128)} %param.10), kind=kLoop, calls=%fused_computation.148 | loop fusion | bytes 160 | tf_op jit(solution)/shard_map/slice | solution.py:14
  1.1 1.6 %fusion.121 = (pred[4]{0:T(512)(128)(4,1)S(1)}, pred[4]{0:T(512)(128)(4,1)S(1)}, pred[4]{0:T(512)(128)(4,1)}, pred[4]{0:T(512)(128)(4,1)S(1)}, pred[4]{0:T(512)(128)(4,1)S(1)}) fusion(s32[5,4]{0,1:T(4,128)} %param.9), kind=kLoop, calls=%fused_computation.152 | loop fusion | flops 20 | bytes 100 | tf_op jit(solution)/shard_map/eq | solution.py:15
  2.7 1.3 %fusion.149 = (bf16[1,2,4,64,128]{4,3,2,1,0:T(8,128)(2,1)S(1)}, bf16[1,2,4,64,128]{4,3,2,1,0:T(8,128)(2,1)S(1)}, bf16[1,2,4,64,128]{4,3,2,1,0:T(8,128)(2,1)S(1)}...) fusion(bf16[5,2,4,64,128]{4,3,2,1,0:T(8,128)(2,1)} %param.8), kind=kLoop, calls=%fused_computation.180 | loop fusion | bytes 1310720 | tf_op jit(solution)/shard_map/slice | solution.py:17
  4.0 0.2 copy.19
  4.2 0.1 fusion.132
  4.3 0.7 slice_bitcast_fusion
  5.0 0.7 fusion.148
  5.7 1.1 %slice_bitcast_fusion.18 = (bf16[4,128,128]{2,1,0:T(8,128)(2,1)}, bf16[4,128,128]{2,1,0:T(8,128)(2,1)}, bf16[4,128,128]{2,1,0:T(8,128)(2,1)}, bf16[4,128,128]{2,...) fusion(bf16[5,2,4,128,128]{4,3,2,1,0:T(8,128)(2,1)S(1)} %copy-d, ...), kind=kLoop, calls=%fused_computation.133 | loop fusion | bytes 2621440 | tf_op jit(solution)/shard_map/squeeze | solution.py:20
  6.8 0.9 %fusion.139 = (bf16[4,128,128]{2,1,0:T(8,128)(2,1)}, bf16[4,128,128]{2,1,0:T(8,128)(2,1)}, bf16[4,128,128]{2,1,0:T(8,128)(2,1)}, bf16[4,128,128]{2,1,0:T(8,128)(2,1)}, bf16[4,128,128]{2,1,0:T(8,128)(2,1)}) fusion(bf16[5,2,4,128,128]{4,3,2,1,0:T(8,128)(2,1)S(1)} %copy-done.1), kind=kLoop, calls=%fused_computation.170 | loop fusion | flops 327680 | bytes 1310720 | tf_op jit(solution)/shard_map/neg | solution.py:20
  7.7 0.2 copy.18
  7.9 0.1 fusion.126
  8.0 0.7 slice_bitcast_fusion.2
  8.8 0.7 fusion.147
  9.4 0.5 convolution_convert_fusion
  9.9 0.1 rev.6
  10.0 2.0 %fusion.32 = bf16[4,256,512]{2,1,0:T(8,128)(2,1)S(1)} fusion(bf16[4,128,512]{2,1,0:T(8,128)(2,1)S(1)} %bitcast.123, bf16[4,256,512]{2,1,0:T(8,128)(2,1)S(1)} %bitcast.118, bf16[4,128,64]{2,1,0:T(8,128)(2,1)} %get-tuple-element.44, bf16[4,128,64]{2,1,0:T(8,128)(2,1)} %get-tuple-element.43, bf16[4,128,128]{2,1,0:T(8,128)(2,1)} %get-tuple-element.29, ...), kind=kOutput, calls=%fused_computation.24 | convolution fusion | flops 412614656 | bytes 3211264 | tf_op jit(solution)/shard_map/bij,bjn->bin/dot_general | solution.py:38
  12.1 0.1 rev.7
  12.2 2.0 %fusion.29 = bf16[4,256,512]{2,1,0:T(8,128)(2,1)S(1)} fusion(bf16[4,128,512]{2,1,0:T(8,128)(2,1)S(1)} %bitcast.124, bf16[4,256,512]{2,1,0:T(8,128)(2,1)S(1)} %fusion.32, bf16[4,128,64]{2,1,0:T(8,128)(2,1)} %get-tuple-element.42, bf16[4,128,64]{2,1,0:T(8,128)(2,1)} %get-tuple-element.41, bf16[4,128,128]{2,1,0:T(8,128)(2,1)} %get-tuple-element.22, ...), kind=kOutput, calls=%fused_computation.23 | convolution fusion | flops 412614656 | bytes 3211264 | tf_op jit(solution)/shard_map/bij,bjn->bin/dot_general | solution.py:38
  14.3 3.0 %collective-permute-start = (bf16[4,2,64,512]{3,2,1,0:T(8,128)(2,1)S(1)}, bf16[4,2,64,512]{3,2,1,0:T(8,128)(2,1)}, u32[]{:S(2)}, u32[]{:S(2)}) collective-permute-start(bf16[4,2,64,512]{3,2,1,0:T(8,128)(2,1)S(1)} %slice.217), channel_id=1, source_target_pairs={{0,2},{2,0},{1,3},{3,1},{4,6},{6,4},{5,7},{7,5},{8,10},{10,8},{9,1... | collective-permute-start | bytes 1572872 | tf_op jit(solution)/shard_map/ppermute | solution.py:8
  17.3 0.2 copy.17
  17.5 0.8 %fusion.120 = (bf16[4,64]{1,0:T(4,128)(2,1)S(1)}, bf16[4,64]{1,0:T(4,128)(2,1)S(1)}) fusion(s32[4]{0:T(128)S(1)} %get-tuple-element.10, pred[4]{0:T(512)(128)(4,1)S(1)} %get-tuple-element.5, pred[4]{0:T(512)(128)(4,1)} %get-tuple-element.7, s32[4]{0:T(128)S(1)} %get-tuple-element.12), kind=kLoop, calls=%fused_computation.151 | loop fusion | flops 1536 | bytes 1064 | tf_op jit(solution)/shard_map/convert_element_type | solution.py:17
  18.3 0.2 copy.16
  18.5 10.8 %collective-permute-done = bf16[4,2,64,512]{3,2,1,0:T(8,128)(2,1)} collective-permute-done((bf16[4,2,64,512]{3,2,1,0:T(8,128)(2,1)S(1)}, bf16[4,2,64,512]{3,2,1,0:T(8,128)(2,1)}, u32[]{:S(2)}, u32[]{:S(2)}) %collective-permute-start) | collective-permute-done | bytes 524320 | tf_op jit(solution)/shard_map/ppermute | solution.py:8
  29.3 2.0 %fusion.26 = bf16[4,256,512]{2,1,0:T(8,128)(2,1)S(1)} fusion(bf16[4,128,512]{2,1,0:T(8,128)(2,1)} %bitcast.42, bf16[4,256,512]{2,1,0:T(8,128)(2,1)S(1)} %copy-done.3, bf16[4,128,64]{2,1,0:T(8,128)(2,1)S(1)} %get-tuple-element.40, bf16[4,128,64]{2,1,0:T(8,128)(2,1)S(1)} %get-tuple-element.39, bf16[4,128,128]{2,1,0:T(8,128)(2,1)} %get-tuple-element.24, ...), kind=kOutput, calls=%fused_computation.22 | convolution fusion | flops 412614656 | bytes 3211264 | tf_op jit(solution)/shard_map/bij,bjn->bin/dot_general | solution.py:38
  31.4 1.9 %collective-permute-start.1 = (bf16[4,2,64,512]{3,2,1,0:T(8,128)(2,1)S(1)}, bf16[4,2,64,512]{3,2,1,0:T(8,128)(2,1)S(1)}, u32[]{:S(2)}, u32[]{:S(2)}) collective-permute-start(bf16[4,2,64,512]{3,2,1,0:T(8,128)(2,1)S(1)} %slice.218), channel_id=1, source_target_pairs={{0,4},{4,0},{8,12},{12,8},{1,5},{5,1},{9,13},{13,9},{2,6},{6,2},{1... | collective-permute-start | bytes 1572872 | tf_op jit(solution)/shard_map/ppermute | solution.py:8
  33.3 0.2 copy.15
  33.6 11.0 %collective-permute-done.1 = bf16[4,2,64,512]{3,2,1,0:T(8,128)(2,1)S(1)} collective-permute-done((bf16[4,2,64,512]{3,2,1,0:T(8,128)(2,1)S(1)}, bf16[4,2,64,512]{3,2,1,0:T(8,128)(2,1)S(1)}, u32[]{:S(2)}, u32[]{:S(2)}) %collective-permute-start.1) | collective-permute-done | bytes 524320 | tf_op jit(solution)/shard_map/ppermute | solution.py:8
  44.6 1.9 %fusion.23 = bf16[4,256,512]{2,1,0:T(8,128)(2,1)S(1)} fusion(bf16[4,128,512]{2,1,0:T(8,128)(2,1)S(1)} %bitcast.128, bf16[4,256,512]{2,1,0:T(8,128)(2,1)} %copy-done.4, bf16[4,128,64]{2,1,0:T(8,128)(2,1)S(1)} %get-tuple-element.38, bf16[4,128,64]{2,1,0:T(8,128)(2,1)S(1)} %get-tuple-element.37, bf16[4,128,128]{2,1,0:T(8,128)(2,1)S(1)} %copy-done.9, ...), kind=kOutput, calls=%fused_computation.21 | convolution fusion | flops 412614656 | bytes 3211264 | tf_op jit(solution)/shard_map/bij,bjn->bin/dot_general | solution.py:38
  46.6 2.6 %collective-permute-start.2 = (bf16[4,2,64,512]{3,2,1,0:T(8,128)(2,1)S(1)}, bf16[4,2,64,512]{3,2,1,0:T(8,128)(2,1)S(1)}, u32[]{:S(2)}, u32[]{:S(2)}) collective-permute-start(bf16[4,2,64,512]{3,2,1,0:T(8,128)(2,1)S(1)} %slice.219), channel_id=1, source_target_pairs={{0,8},{4,12},{8,0},{12,4},{1,9},{5,13},{9,1},{13,5},{2,10},{6,14},... | collective-permute-start | bytes 1572872 | tf_op jit(solution)/shard_map/ppermute | solution.py:8
  49.3 21.7 %collective-permute-done.2 = bf16[4,2,64,512]{3,2,1,0:T(8,128)(2,1)S(1)} collective-permute-done((bf16[4,2,64,512]{3,2,1,0:T(8,128)(2,1)S(1)}, bf16[4,2,64,512]{3,2,1,0:T(8,128)(2,1)S(1)}, u32[]{:S(2)}, u32[]{:S(2)}) %collective-permute-start.2) | collective-permute-done | bytes 524320 | tf_op jit(solution)/shard_map/ppermute | solution.py:8
  71.0 0.7 %fusion.20 = bf16[4,256,512]{2,1,0:T(8,128)(2,1)S(1)} fusion(bf16[4,128,512]{2,1,0:T(8,128)(2,1)S(1)} %bitcast.129, bf16[4,256,512]{2,1,0:T(8,128)(2,1)S(1)} %fusion.23, bf16[4,128,64]{2,1,0:T(8,128)(2,1)S(1)} %get-tuple-element.36, bf16[4,128,64]{2,1,0:T(8,128)(2,1)S(1)} %get-tuple-element.35, bf16[4,128,128]{2,1,0:T(8,128)(2,1)S(1)} %copy-done.6, ...), kind=kOutput, calls=%fused_computation.20 | convolution fusion | flops 412614656 | bytes 3211264 | tf_op jit(solution)/shard_map/bij,bjn->bin/dot_general | solution.py:38
  71.8 1.1 %copy.13 = bf16[2,4,128,512]{3,2,1,0:T(8,128)(2,1)} copy(bf16[2,4,128,512]{3,2,0,1:T(8,128)(2,1)S(1)} %bitcast.122) | data formatting | bytes 2097152 | tf_op jit(solution)/shard_map/transpose | solution.py:77
  (40 shorter events, 0.5 us)
Async XLA Ops:
  0.0 9.4 %copy-start = (bf16[2,512,512]{2,1,0:T(8,128)(2,1)S(1)}, bf16[2,512,512]{2,1,0:T(8,128)(2,1)}, u32[]{:S(2)}) copy-start(bf16[2,512,512]{2,1,0:T(8,128)(2,1)} %param.6) | copy-start | bytes 3145732
  2.7 3.0 %copy-start.1 = (bf16[5,2,4,128,128]{4,3,2,1,0:T(8,128)(2,1)S(1)}, bf16[5,2,4,128,128]{4,3,2,1,0:T(8,128)(2,1)}, u32[]{:S(2)}) copy-start(bf16[5,2,4,128,128]{4,3,2,1,0:T(8,128)(2,1)} %param.7) | copy-start | bytes 3932164
  6.8 2.6 %copy-start.11 = (s32[4,128]{1,0:T(4,128)S(1)}, s32[4,128]{1,0:T(4,128)}, u32[]{:S(2)}) copy-start(s32[4,128]{1,0:T(4,128)} %param.11) | copy-start | bytes 6148
  14.2 3.1 %copy-start.2 = (bf16[4,256,512]{2,1,0:T(8,128)(2,1)}, bf16[4,256,512]{2,1,0:T(8,128)(2,1)S(1)}, u32[]{:S(2)}) copy-start(bf16[4,256,512]{2,1,0:T(8,128)(2,1)S(1)} %fusion.29) | copy-start | bytes 3145732
  14.3 15.0 %collective-permute-start = (bf16[4,2,64,512]{3,2,1,0:T(8,128)(2,1)S(1)}, bf16[4,2,64,512]{3,2,1,0:T(8,128)(2,1)}, u32[]{:S(2)}, u32[]{:S(2)}) collective-permute-start(bf16[4,2,64,512]{3,2,1,0:T(8,128)(2,1)S(1)} %slice.217), channel_id=1, source_target_pairs={{0,2},{2,0},{1,3},{3,1},{4,6},{6,4},{5,7},{7,5},{8,10},{10,8},{9,1... | collective-permute-start | bytes 1572872 | tf_op jit(solution)/shard_map/ppermute | solution.py:8
  17.3 12.0 %copy-start.3 = (bf16[4,256,512]{2,1,0:T(8,128)(2,1)S(1)}, bf16[4,256,512]{2,1,0:T(8,128)(2,1)}, u32[]{:S(2)}) copy-start(bf16[4,256,512]{2,1,0:T(8,128)(2,1)} %copy-done.2) | copy-start | bytes 3145732
  31.3 2.0 %copy-start.4 = (bf16[4,256,512]{2,1,0:T(8,128)(2,1)}, bf16[4,256,512]{2,1,0:T(8,128)(2,1)S(1)}, u32[]{:S(2)}) copy-start(bf16[4,256,512]{2,1,0:T(8,128)(2,1)S(1)} %fusion.26) | copy-start | bytes 3145732
  31.3 13.3 %copy-start.8 = (bf16[4,128,128]{2,1,0:T(8,128)(2,1)S(1)}, bf16[4,128,128]{2,1,0:T(8,128)(2,1)}, u32[]{:S(2)}) copy-start(bf16[4,128,128]{2,1,0:T(8,128)(2,1)} %get-tuple-element.25) | copy-start | bytes 393220
  31.3 13.3 %copy-start.9 = (bf16[4,128,128]{2,1,0:T(8,128)(2,1)S(1)}, bf16[4,128,128]{2,1,0:T(8,128)(2,1)}, u32[]{:S(2)}) copy-start(bf16[4,128,128]{2,1,0:T(8,128)(2,1)} %get-tuple-element.26) | copy-start | bytes 393220
  31.3 13.2 %copy-start.10 = (bf16[4,128,128]{2,1,0:T(8,128)(2,1)S(1)}, bf16[4,128,128]{2,1,0:T(8,128)(2,1)}, u32[]{:S(2)}) copy-start(bf16[4,128,128]{2,1,0:T(8,128)(2,1)} %get-tuple-element.19) | copy-start | bytes 393220
  31.4 13.2 %collective-permute-start.1 = (bf16[4,2,64,512]{3,2,1,0:T(8,128)(2,1)S(1)}, bf16[4,2,64,512]{3,2,1,0:T(8,128)(2,1)S(1)}, u32[]{:S(2)}, u32[]{:S(2)}) collective-permute-start(bf16[4,2,64,512]{3,2,1,0:T(8,128)(2,1)S(1)} %slice.218), channel_id=1, source_target_pairs={{0,4},{4,0},{8,12},{12,8},{1,5},{5,1},{9,13},{13,9},{2,6},{6,2},{1... | collective-permute-start | bytes 1572872 | tf_op jit(solution)/shard_map/ppermute | solution.py:8
  46.5 24.5 %copy-start.5 = (bf16[4,128,128]{2,1,0:T(8,128)(2,1)S(1)}, bf16[4,128,128]{2,1,0:T(8,128)(2,1)}, u32[]{:S(2)}) copy-start(bf16[4,128,128]{2,1,0:T(8,128)(2,1)} %get-tuple-element.20) | copy-start | bytes 393220
  46.6 24.5 %copy-start.6 = (bf16[4,128,128]{2,1,0:T(8,128)(2,1)S(1)}, bf16[4,128,128]{2,1,0:T(8,128)(2,1)}, u32[]{:S(2)}) copy-start(bf16[4,128,128]{2,1,0:T(8,128)(2,1)} %get-tuple-element.27) | copy-start | bytes 393220
  46.6 24.4 %copy-start.7 = (bf16[4,128,128]{2,1,0:T(8,128)(2,1)S(1)}, bf16[4,128,128]{2,1,0:T(8,128)(2,1)}, u32[]{:S(2)}) copy-start(bf16[4,128,128]{2,1,0:T(8,128)(2,1)} %get-tuple-element.15) | copy-start | bytes 393220
  46.6 24.4 %collective-permute-start.2 = (bf16[4,2,64,512]{3,2,1,0:T(8,128)(2,1)S(1)}, bf16[4,2,64,512]{3,2,1,0:T(8,128)(2,1)S(1)}, u32[]{:S(2)}, u32[]{:S(2)}) collective-permute-start(bf16[4,2,64,512]{3,2,1,0:T(8,128)(2,1)S(1)} %slice.219), channel_id=1, source_target_pairs={{0,8},{4,12},{8,0},{12,4},{1,9},{5,13},{9,1},{13,5},{2,10},{6,14},... | collective-permute-start | bytes 1572872 | tf_op jit(solution)/shard_map/ppermute | solution.py:8

commit v2 on v1

v2 whole, which is shorter than its diff:
```python
import functools

import jax
import jax.numpy as jnp
from jax import lax
from jax.experimental import pallas as pl
from jax.experimental.pallas import tpu as pltpu
from jax.sharding import PartitionSpec as P

MESH = pl.DeviceIdType.MESH
WIDTH = 256
LAG = 2


def remote_levels():
    steps = []
    for axis in ("sub", "leaf"):
        for which_bit in range(lax.axis_size(axis).bit_length() - 1):
            steps.append((axis, 2**which_bit))
    return steps


def partner_of(axis, stride):
    me = lax.axis_index(axis)
    return {axis: me + stride * (1 - 2 * ((me // stride) % 2))}


def kernel(
    remote,
    ranks_ref,
    coupling_ref,
    order_ref,
    incident_ref,
    self_ref,
    cross_ref,
    out_ref,
    panel,
    weight,
    cross,
    own_matrix,
    cross_matrix,
    field,
    arrived,
    result,
    panel_sem,
    weight_sem,
    cross_sem,
    send_sem,
    recv_sem,
    out_sem,
):
    n_levels, _, blocks, rows, _ = weight.shape
    lead = cross.shape[3]
    chunks = panel.shape[0]
    width = panel.shape[4]
    local = n_levels - len(remote)
    partners = [partner_of(axis, stride) for axis, stride in remote]

    barrier = pltpu.get_barrier_semaphore()
    for partner in partners:
        pl.semaphore_signal(barrier, inc=1, device_id=partner, device_id_type=MESH)

    def load_panel(chunk):
        columns = pl.ds(chunk * width, width)
        return [
            pltpu.make_async_copy(
                incident_ref.at[:, pl.ds(block * rows, rows), columns],
                panel.at[chunk, block],
                panel_sem.at[chunk, block],
            )
            for block in range(blocks)
        ]

    def load_weight(level):
        return [
            pltpu.make_async_copy(self_ref.at[level], weight.at[level], weight_sem.at[level]),
            pltpu.make_async_copy(cross_ref.at[level], cross.at[level], cross_sem.at[level]),
        ]

    panels = [load_panel(chunk) for chunk in range(chunks)]
    weights = [load_weight(level) for level in range(n_levels)]
    for copy in panels[0]:
        copy.start()
    for level in range(local):
        for copy in weights[level]:
            copy.start()
    for chunk in range(1, chunks):
        for copy in panels[chunk]:
            copy.start()
    for level in range(local, n_levels):
        for copy in weights[level]:
            copy.start()

    row_index = lax.broadcasted_iota(jnp.int32, (lead, rows), 0)

    def prepare(level):
        for copy in weights[level]:
            copy.wait()
        for block in range(blocks):
            own_real = weight[level, 0, block]
            own_imag = weight[level, 1, block]
            own_matrix[level, block, :rows, :rows] = own_real
            own_matrix[level, block, :rows, rows:] = -own_imag
            own_matrix[level, block, rows:, :rows] = own_imag
            own_matrix[level, block, rows:, rows:] = own_real
            rank = jnp.where(coupling_ref[level, block] == 1, ranks_ref[level, block], 0)
            coupled = (row_index < rank).astype(jnp.float32)
            real = cross[level, 0, block].astype(jnp.float32) * coupled
            imag = cross[level, 1, block].astype(jnp.float32) * coupled
            cross_matrix[level, block, :rows] = jnp.concatenate([real, -imag], axis=0).T.astype(
                jnp.bfloat16
            )
            cross_matrix[level, block, rows:] = jnp.concatenate([imag, real], axis=0).T.astype(
                jnp.bfloat16
            )

    def apply(level, block, own, sibling):
        own = own.reshape(2 * rows, width)
        sibling = sibling.reshape(2 * lead, width)
        total = jnp.dot(own_matrix[level, block], own, preferred_element_type=jnp.float32)
        total += jnp.dot(cross_matrix[level, block], sibling, preferred_element_type=jnp.float32)
        return total.astype(jnp.bfloat16).reshape(2, rows, width)

    def send(step, chunk, block):
        return pltpu.make_async_remote_copy(
            src_ref=field.at[local + step, chunk, block, :, pl.ds(0, lead), :],
            dst_ref=arrived.at[step, chunk, block],
            send_sem=send_sem.at[step, chunk, block],
            recv_sem=recv_sem.at[step, chunk, block],
            device_id=partners[step],
            device_id_type=MESH,
        )

    def store_out(chunk, block):
        return pltpu.make_async_copy(
            result.at[chunk, block],
            out_ref.at[:, pl.ds(block * rows, rows), pl.ds(chunk * width, width)],
            out_sem.at[chunk, block],
        )

    selectors = []
    square = lax.broadcasted_iota(jnp.int32, (rows, rows), 0)
    for block in range(blocks):
        picked = square == order_ref[pl.ds(block, 1), :]
        selectors.append(picked.astype(jnp.float32).T.astype(jnp.bfloat16))

    for chunk in range(chunks):
        for block in range(blocks):
            panels[chunk][block].wait()
            for part in range(2):
                field[0, chunk, block, part] = jnp.dot(
                    selectors[block], panel[chunk, block, part], preferred_element_type=jnp.float32
                ).astype(jnp.bfloat16)
        for level in range(local):
            if chunk == 0:
                prepare(level)
            for block in range(blocks):
                field[level + 1, chunk, block] = apply(
                    level,
                    block,
                    field[level, chunk, block],
                    field[level, chunk, block ^ 2**level, :, :lead],
                )
                if level == local - 1:
                    if chunk == 0 and block == 0:
                        pl.semaphore_wait(barrier, len(partners))
                    send(0, chunk, block).start()
    for level in range(local, n_levels):
        prepare(level)

    def advance(step, unit):
        chunk, block = unit // blocks, unit % blocks
        level = local + step
        send(step, chunk, block).wait_recv()
        new = apply(level, block, field[level, chunk, block], arrived[step, chunk, block])
        if step < len(remote) - 1:
            field[level + 1, chunk, block] = new
            send(step + 1, chunk, block).start()
        else:
            result[chunk, block] = new
            store_out(chunk, block).start()

    units = chunks * blocks
    for turn in range(units + LAG * (len(remote) - 1)):
        for step in range(len(remote)):
            unit = turn - LAG * step
            if 0 <= unit < units:
                advance(step, unit)
    for chunk in range(chunks):
        for block in range(blocks):
            for step in range(len(remote)):
                send(step, chunk, block).wait_send()
            store_out(chunk, block).wait()


def shards(incident, self_weight, cross_weight, coupling, block_ranks, leaf_order):
    n_levels, _, blocks, rows, _ = self_weight.shape
    lead = cross_weight.shape[3]
    columns = incident.shape[2]
    width = min(WIDTH, columns)
    chunks = columns // width
    remote = remote_levels()
    far = len(remote)
    smem = pl.BlockSpec(memory_space=pltpu.SMEM)
    vmem = pl.BlockSpec(memory_space=pltpu.VMEM)
    anywhere = pl.BlockSpec(memory_space=pl.ANY)
    bf16 = jnp.bfloat16
    return pl.pallas_call(
        functools.partial(kernel, remote),
        out_shape=jax.ShapeDtypeStruct(incident.shape, bf16),
        in_specs=[smem, smem, vmem, anywhere, anywhere, anywhere],
        out_specs=anywhere,
        scratch_shapes=[
            pltpu.VMEM((chunks, blocks, 2, rows, width), bf16),
            pltpu.VMEM((n_levels, 2, blocks, rows, rows), bf16),
            pltpu.VMEM((n_levels, 2, blocks, lead, rows), bf16),
            pltpu.VMEM((n_levels, blocks, 2 * rows, 2 * rows), bf16),
            pltpu.VMEM((n_levels, blocks, 2 * rows, 2 * lead), bf16),
            pltpu.VMEM((n_levels, chunks, blocks, 2, rows, width), bf16),
            pltpu.VMEM((far, chunks, blocks, 2, lead, width), bf16),
            pltpu.VMEM((chunks, blocks, 2, rows, width), bf16),
            pltpu.SemaphoreType.DMA((chunks, blocks)),
            pltpu.SemaphoreType.DMA((n_levels,)),
            pltpu.SemaphoreType.DMA((n_levels,)),
            pltpu.SemaphoreType.DMA((far, chunks, blocks)),
            pltpu.SemaphoreType.DMA((far, chunks, blocks)),
            pltpu.SemaphoreType.DMA((chunks, blocks)),
        ],
        compiler_params=pltpu.CompilerParams(
            collective_id=0, has_side_effects=True, vmem_limit_bytes=48 * 2**20
        ),
    )(block_ranks, coupling, leaf_order, incident, self_weight, cross_weight)


def solution(mesh):
    in_specs = (
        P(None, ("leaf", "sub"), ("groups", "col")),
        P("groups", None, ("leaf", "sub"), None, None),
        P("groups", None, ("leaf", "sub"), None, None),
        P("groups", ("leaf", "sub")),
        P("groups", ("leaf", "sub")),
        P(("groups", "leaf", "sub"), None),
    )
    out_specs = P(None, ("leaf", "sub"), ("groups", "col"))
    return jax.shard_map(shards, mesh=mesh, in_specs=in_specs, out_specs=out_specs, check_vma=False)
```

time: 73.1 us -> 46.5 us (0.64)
  waiting for transfers between devices: 43.5 us -> 0 us
  Pallas kernels: 0 us -> 39.4 us
  matrix products: 9.16 us -> 0 us
  starting transfers between devices: 7.47 us -> 0 us
  other arithmetic: 4.92 us -> 0 us
    ppermute x3 -> x0, waiting for transfers between devices: 43.5 us -> none  [from_partner(): lax.ppermute(x, axis, [(i, i ^ 1 << stride) for i in range(lax.axis_size(...]
    pallas_call x0 -> x1, Pallas kernels: none -> 39.4 us  [shards(): pl.pallas_call(functools.partial(kernel, remote), out_shape=jax.ShapeDtyp...]
    dot_general x6 -> x0, matrix products: 9.16 us -> none  [the longest x5 8.68 us: apply_level(): jnp.einsum('bij,bjn->bin', matrix, stacked, preferred_element_type=jnp.fl...]
    ppermute x3 -> x0, starting transfers between devices: 7.47 us -> none  [from_partner(): lax.ppermute(x, axis, [(i, i ^ 1 << stride) for i in range(lax.axis_size(...]
    unnamed x29 -> x11, local copies, waits for them, and re-layouts: 0.94 us -> 6.81 us
    slice x7 -> x0, local copies, waits for them, and re-layouts: 2.64 us -> none  [the longest x1 1.32 us: level_matrix(): cross_weight[level_index] * coupled[None, :, :, None].astype(jnp.bfloat16)]
    squeeze x6 -> x0, local copies, waits for them, and re-layouts: 2.63 us -> none  [level_matrix(): upper = jnp.concatenate([own[0], -own[1], cross_t[0], -cross_t[1]], axis=2)]
    neg x6 -> x0, other arithmetic: 2.29 us -> none  [level_matrix(): upper = jnp.concatenate([own[0], -own[1], cross_t[0], -cross_t[1]], axis=2)]
  transfers between devices with their start and end apart: 3 -> 0, of which waited for: 3 -> 0; matrix products, arithmetic and copies ran while one was open for 2% -> 0% of each run, Pallas kernels for 0% -> 0%
where the time goes in v2:
time: 46.5 us; the launch traced here: 46.2 us
  Pallas kernels  39.4 us (85%)
  local copies, waits for them, and re-layouts  6.81 us (15%)
    pallas_call x1, Pallas kernels, shards(): pl.pallas_call(functools.partial(kernel, remote), out_shape=jax.ShapeDtyp...  39.4 us
    unnamed x11, local copies, waits for them, and re-layouts  6.81 us

profile of v2, /device:TPU:0, one launch (start us, length us, event | category | flops | bytes accessed | tf_op | source)
XLA Modules:
  0.0 46.2 jit_solution(5211250517711760492)
XLA Ops:
  0.0 0.8 %copy.8.coupling_ref = s32[5,4]{1,0:T(8,128)S(1)} copy(s32[5,4]{0,1:T(4,128)} %param.9) | data formatting | bytes 160 | tf_op args[3]
  0.8 0.8 %copy.7.ranks_ref = s32[5,4]{1,0:T(8,128)S(1)} copy(s32[5,4]{0,1:T(4,128)} %param.10) | data formatting | bytes 160 | tf_op args[4]
  1.5 0.0 copy-start
  1.5 1.3 %copy-done = bf16[5,2,4,128,128]{4,3,2,1,0:T(8,128)(2,1)S(1)} copy-done((bf16[5,2,4,128,128]{4,3,2,1,0:T(8,128)(2,1)S(1)}, bf16[5,2,4,128,128]{4,3,2,1,0:T(8,128)(2,1)}, u32[]{:S(2)}) %copy-start) | copy-done | bytes 1310744
  2.9 0.0 copy-start.1
  2.9 1.2 %copy-done.1 = bf16[2,512,512]{2,1,0:T(8,128)(2,1)S(1)} copy-done((bf16[2,512,512]{2,1,0:T(8,128)(2,1)S(1)}, bf16[2,512,512]{2,1,0:T(8,128)(2,1)}, u32[]{:S(2)}) %copy-start.1) | copy-done | bytes 1048600
  4.1 0.0 copy-start.2
  4.1 1.1 %copy-done.2 = bf16[5,2,4,64,128]{4,3,2,1,0:T(8,128)(2,1)S(1)} copy-done((bf16[5,2,4,64,128]{4,3,2,1,0:T(8,128)(2,1)S(1)}, bf16[5,2,4,64,128]{4,3,2,1,0:T(8,128)(2,1)}, u32[]{:S(2)}) %copy-start.2) | copy-done | bytes 655384
  5.2 0.0 copy-start.3
  5.2 0.7 %copy-done.3 = s32[4,128]{1,0:T(4,128)S(1)} copy-done((s32[4,128]{1,0:T(4,128)S(1)}, s32[4,128]{1,0:T(4,128)}, u32[]{:S(2)}) %copy-start.3) | copy-done | bytes 2072
  5.8 39.4 %shard_map.64 = bf16[2,512,512]{2,1,0:T(8,128)(2,1)S(1)} custom-call(s32[5,4]{1,0:T(8,128)S(1)} %copy.7.ranks_ref, s32[5,4]{1,0:T(8,128)S(1)} %copy.8.coupling_ref, s32[4,128]{1,0:T(4,128)S(1)} %copy-done.3, bf16[2,512,512]{2,1,0:T(8,128)(2,1)S(1)} %copy-done.1, bf16[5,2,4,128,128]{4,3,2,1,0:T(8,128)(2,1)S(1)} %copy-done, ...), custom_call_target="tpu_custom_call" | custom-call | tf_op jit(solution)/shard_map/pallas_call | solution.py:208
  45.3 1.0 %copy.10 = bf16[2,512,512]{2,1,0:T(8,128)(2,1)} copy(bf16[2,512,512]{2,1,0:T(8,128)(2,1)S(1)} %shard_map.64) | data formatting | bytes 2097152
Async XLA Ops:
  1.5 1.3 %copy-start = (bf16[5,2,4,128,128]{4,3,2,1,0:T(8,128)(2,1)S(1)}, bf16[5,2,4,128,128]{4,3,2,1,0:T(8,128)(2,1)}, u32[]{:S(2)}) copy-start(bf16[5,2,4,128,128]{4,3,2,1,0:T(8,128)(2,1)} %self_ref.1) | copy-start | bytes 3932164
  2.9 1.2 %copy-start.1 = (bf16[2,512,512]{2,1,0:T(8,128)(2,1)S(1)}, bf16[2,512,512]{2,1,0:T(8,128)(2,1)}, u32[]{:S(2)}) copy-start(bf16[2,512,512]{2,1,0:T(8,128)(2,1)} %incident_ref.1) | copy-start | bytes 3145732
  4.1 1.1 %copy-start.2 = (bf16[5,2,4,64,128]{4,3,2,1,0:T(8,128)(2,1)S(1)}, bf16[5,2,4,64,128]{4,3,2,1,0:T(8,128)(2,1)}, u32[]{:S(2)}) copy-start(bf16[5,2,4,64,128]{4,3,2,1,0:T(8,128)(2,1)} %cross_ref.1) | copy-start | bytes 1966084
  5.2 0.7 %copy-start.3 = (s32[4,128]{1,0:T(4,128)S(1)}, s32[4,128]{1,0:T(4,128)}, u32[]{:S(2)}) copy-start(s32[4,128]{1,0:T(4,128)} %order_ref.1) | copy-start | bytes 6148

commit v3 on v2

--- a/solution.py
+++ b/solution.py
@@ -9,7 +9,9 @@
 
 MESH = pl.DeviceIdType.MESH
 WIDTH = 256
-LAG = 2
+LAG = 1
+TAIL = 4
+AHEAD = 3
 
 
 def remote_levels():
@@ -41,13 +43,11 @@
     cross_matrix,
     field,
     arrived,
-    result,
     panel_sem,
     weight_sem,
     cross_sem,
     send_sem,
     recv_sem,
-    out_sem,
 ):
     n_levels, _, blocks, rows, _ = weight.shape
     lead = cross.shape[3]
@@ -91,7 +91,9 @@
         for copy in weights[level]:
             copy.start()
 
-    row_index = lax.broadcasted_iota(jnp.int32, (lead, rows), 0)
+    row_index = lax.broadcasted_iota(jnp.int32, (2 * lead, rows), 0)
+    imag_half = lax.broadcasted_iota(jnp.int32, (rows, 2 * lead), 1) >= lead
+    sign = jnp.where(imag_half, -1.0, 1.0).astype(jnp.bfloat16)
 
     def prepare(level):
         for copy in weights[level]:
@@ -103,16 +105,13 @@
             own_matrix[level, block, :rows, rows:] = -own_imag
             own_matrix[level, block, rows:, :rows] = own_imag
             own_matrix[level, block, rows:, rows:] = own_real
-            rank = jnp.where(coupling_ref[level, block] == 1, ranks_ref[level, block], 0)
-            coupled = (row_index < rank).astype(jnp.float32)
-            real = cross[level, 0, block].astype(jnp.float32) * coupled
-            imag = cross[level, 1, block].astype(jnp.float32) * coupled
-            cross_matrix[level, block, :rows] = jnp.concatenate([real, -imag], axis=0).T.astype(
-                jnp.bfloat16
-            )
-            cross_matrix[level, block, rows:] = jnp.concatenate([imag, real], axis=0).T.astype(
-                jnp.bfloat16
-            )
+            at = (pl.ds(block, 1), pl.ds(level, 1))
+            rank = jnp.where(coupling_ref[at] == 1, ranks_ref[at], 0)
+            coupled = (row_index % lead < rank).astype(jnp.float32).astype(jnp.bfloat16)
+            both = jnp.concatenate([cross[level, 0, block], cross[level, 1, block]], axis=0)
+            both = (both * coupled).T
+            cross_matrix[level, block, :rows] = both * sign
+            cross_matrix[level, block, rows:] = jnp.concatenate([both[:, lead:], both[:, :lead]], axis=1)
 
     def apply(level, block, own, sibling):
         own = own.reshape(2 * rows, width)
@@ -129,13 +128,6 @@
             recv_sem=recv_sem.at[step, chunk, block],
             device_id=partners[step],
             device_id_type=MESH,
-        )
-
-    def store_out(chunk, block):
-        return pltpu.make_async_copy(
-            result.at[chunk, block],
-            out_ref.at[:, pl.ds(block * rows, rows), pl.ds(chunk * width, width)],
-            out_sem.at[chunk, block],
         )
 
     selectors = []
@@ -164,33 +156,36 @@
                 if level == local - 1:
                     if chunk == 0 and block == 0:
                         pl.semaphore_wait(barrier, len(partners))
-                    send(0, chunk, block).start()
-    for level in range(local, n_levels):
-        prepare(level)
-
+                    if chunk * blocks + block < AHEAD:
+                        send(0, chunk, block).start()
     def advance(step, unit):
         chunk, block = unit // blocks, unit % blocks
         level = local + step
+        if unit == 0:
+            prepare(level)
         send(step, chunk, block).wait_recv()
         new = apply(level, block, field[level, chunk, block], arrived[step, chunk, block])
         if step < len(remote) - 1:
             field[level + 1, chunk, block] = new
             send(step + 1, chunk, block).start()
         else:
-            result[chunk, block] = new
-            store_out(chunk, block).start()
+            columns = pl.ds(chunk * width, width)
+            out_ref[:, pl.ds(block * rows, rows), columns] = new
 
     units = chunks * blocks
-    for turn in range(units + LAG * (len(remote) - 1)):
+    last = len(remote) - 1
+    lags = [LAG * step + (TAIL if step == last else 0) for step in range(len(remote))]
+    for turn in range(units + lags[last]):
         for step in range(len(remote)):
-            unit = turn - LAG * step
+            unit = turn - lags[step]
             if 0 <= unit < units:
                 advance(step, unit)
+        if turn + AHEAD < units:
+            send(0, (turn + AHEAD) // blocks, (turn + AHEAD) % blocks).start()
     for chunk in range(chunks):
         for block in range(blocks):
             for step in range(len(remote)):
                 send(step, chunk, block).wait_send()
-            store_out(chunk, block).wait()
 
 
 def shards(incident, self_weight, cross_weight, coupling, block_ranks, leaf_order):
@@ -201,15 +196,14 @@
     chunks = columns // width
     remote = remote_levels()
     far = len(remote)
-    smem = pl.BlockSpec(memory_space=pltpu.SMEM)
     vmem = pl.BlockSpec(memory_space=pltpu.VMEM)
-    anywhere = pl.BlockSpec(memory_space=pl.ANY)
+    hbm = pl.BlockSpec(memory_space=pltpu.HBM)
     bf16 = jnp.bfloat16
     return pl.pallas_call(
         functools.partial(kernel, remote),
-        out_shape=jax.ShapeDtypeStruct(incident.shape, bf16),
-        in_specs=[smem, smem, vmem, anywhere, anywhere, anywhere],
-        out_specs=anywhere,
+        out_shape=pltpu.VMEM(incident.shape, bf16),
+        in_specs=[vmem, vmem, vmem, hbm, hbm, hbm],
+        out_specs=vmem,
         scratch_shapes=[
             pltpu.VMEM((chunks, blocks, 2, rows, width), bf16),
             pltpu.VMEM((n_levels, 2, blocks, rows, rows), bf16),
@@ -218,18 +212,16 @@
             pltpu.VMEM((n_levels, blocks, 2 * rows, 2 * lead), bf16),
             pltpu.VMEM((n_levels, chunks, blocks, 2, rows, width), bf16),
             pltpu.VMEM((far, chunks, blocks, 2, lead, width), bf16),
-            pltpu.VMEM((chunks, blocks, 2, rows, width), bf16),
             pltpu.SemaphoreType.DMA((chunks, blocks)),
             pltpu.SemaphoreType.DMA((n_levels,)),
             pltpu.SemaphoreType.DMA((n_levels,)),
             pltpu.SemaphoreType.DMA((far, chunks, blocks)),
             pltpu.SemaphoreType.DMA((far, chunks, blocks)),
-            pltpu.SemaphoreType.DMA((chunks, blocks)),
         ],
         compiler_params=pltpu.CompilerParams(
-            collective_id=0, has_side_effects=True, vmem_limit_bytes=48 * 2**20
+            collective_id=0, has_side_effects=True, vmem_limit_bytes=60 * 2**20
         ),
-    )(block_ranks, coupling, leaf_order, incident, self_weight, cross_weight)
+    )(block_ranks.T, coupling.T, leaf_order, incident, self_weight, cross_weight)
 
 
 def solution(mesh):

time: 46.5 us -> 39.4 us (0.85)
  local copies, waits for them, and re-layouts: 6.81 us -> 0.97 us
  Pallas kernels: 39.4 us -> 38.2 us
    unnamed x11 -> x1, local copies, waits for them, and re-layouts: 6.81 us -> 0.97 us
    pallas_call x1, Pallas kernels: 39.4 us -> 38.2 us  [shards(): pl.pallas_call(functools.partial(kernel, remote), out_shape=pltpu.VMEM(in...]
where the time goes in v3:
time: 39.4 us; the launch traced here: 39.2 us
  Pallas kernels  38.2 us (97%)
  local copies, waits for them, and re-layouts  0.97 us (2%)
    pallas_call x1, Pallas kernels, shards(): pl.pallas_call(functools.partial(kernel, remote), out_shape=pltpu.VMEM(in...  38.2 us
    unnamed x1, local copies, waits for them, and re-layouts  0.97 us

profile of v3, /device:TPU:0, one launch (start us, length us, event | category | flops | bytes accessed | tf_op | source)
XLA Modules:
  0.0 39.2 jit_solution(11090491863689879945)
XLA Ops:
  0.0 38.2 %shard_map.64 = bf16[2,512,512]{2,1,0:T(8,128)(2,1)S(1)} custom-call(s32[4,5]{1,0:T(4,128)} %bitcast.2, s32[4,5]{1,0:T(4,128)} %bitcast.3, s32[4,128]{1,0:T(4,128)} %order_ref.1, bf16[2,512,512]{2,1,0:T(8,128)(2,1)} %incident_ref.1, bf16[5,2,4,128,128]{4,3,2,1,0:T(8,128)(2,1)} %self_ref.1, bf16[5,2,4,64,128]{4,3,2,1,0:T(8,128)(2,1)} %cross_ref.1), custom_call_target="tpu_custom_call" | custom-call | tf_op jit(solution)/shard_map/pallas_call | solution.py:202
  38.2 1.0 %copy.8 = bf16[2,512,512]{2,1,0:T(8,128)(2,1)} copy(bf16[2,512,512]{2,1,0:T(8,128)(2,1)S(1)} %shard_map.64) | data formatting | bytes 2097152
